TPU v7x, 256 devices: a whole 4x4x8 slice. The times are simulated.
256 devices in a mesh: fibre: 8 (over z), cols: 32 (over y, x, core).
Axes of the slice: x: 4, y: 4, z: 8, core: 2. Of those that a mesh axis runs over, the one named last changes fastest.
Arguments:
- tensor: float32 [512, 32, 8, 2048], P('fibre', 'cols'), may hold values from -6 to 6
- initial: float32 [512, 64], replicated, may hold values from -6 to 6
Outputs:
- core_slab: float32 [64, 32, 8, 2048], P(None, 'cols', 'fibre')
- basis: float32 [512, 64], replicated
All inputs are finite; a program needn't handle non-finite values.
Results may differ from a plain program's by a relative error of at most 0.0002.
Values sent between devices are 32-bit elements; how exact they have to be, the bound alone decides.
A program may use at most 64 MiB of HBM per device.

v0:
```python
import jax
import jax.numpy as jnp
from jax import lax
from jax.sharding import PartitionSpec as P

ITERS = 2


def orthonormal(product):
    squares = jnp.dot(product.T, product, precision=lax.Precision.HIGHEST)
    lower = jnp.linalg.cholesky(squares)
    return lax.linalg.triangular_solve(
        lower, product, left_side=False, lower=True, transpose_a=True
    )


def shards(tensor, initial):
    highest = lax.Precision.HIGHEST
    gathered = lax.all_to_all(tensor, "fibre", split_axis=2, concat_axis=0, tiled=True)
    modes = gathered.shape[0]
    width = gathered.shape[3]
    columns = gathered.reshape(modes, width)
    local_gram = jnp.dot(columns, columns.T, precision=highest)
    gram = lax.psum(local_gram, ("fibre", "cols"))
    basis = initial
    for step in range(ITERS):
        basis = orthonormal(jnp.dot(gram, basis, precision=highest))
    ranks = basis.shape[1]
    core_slab = jnp.dot(basis.T, columns, precision=highest).reshape(ranks, 1, 1, width)
    return (core_slab, basis)


def solution(mesh):
    placed = (P("fibre", "cols", None, None), P())
    return jax.shard_map(
        shards,
        mesh=mesh,
        in_specs=placed,
        out_specs=(P(None, "cols", "fibre", None), P()),
        check_vma=False,
    )
```

profile of v0, /device:TPU:1, one launch (start us, length us, event | category | flops | bytes accessed | tf_op | source)
XLA Modules:
  0.0 421.4 jit_solution(10958943647922258602)
XLA Ops:
  7.2 0.0 copy-start
  7.2 0.0 all-reduce.2.cloned.1.call-start
  7.2 4.6 %copy.11 = f32[64,1,8,2048]{3,0,1,2:T(8,128)S(1)} copy(f32[64,1,8,2048]{3,2,1,0:T(8,128)} %param.5) | data formatting | bytes 8388608 | tf_op args[0]
  11.9 103.5 %all_to_all.15 = f32[64,1,8,2048]{3,0,1,2:T(8,128)S(1)} all-to-all(f32[64,1,8,2048]{3,0,1,2:T(8,128)S(1)} %copy.11), channel_id=1, replica_groups=mesh['fibre'=8,'cols'=32] {'fibre'}, dimensions={2} | all-to-all | bytes 8388608 | tf_op jit(solution)/shard_map/all_to_all | solution.py:19
  115.3 0.0 copy-start.1
  115.3 1.9 copy-done.1
  117.3 7.9 %fusion.8 = f32[512,512]{1,0:T(8,128)} fusion(f32[512,2048]{1,0:T(8,128)S(1)} %bitcast.43), kind=kOutput, calls=%fused_computation.20 | convolution fusion | flops 6442450944 | bytes 5242880 | tf_op jit(solution)/shard_map/dot_general | solution.py:23
  125.2 0.0 all-reduce.2.cloned.1.call-update
  125.2 252.7 %all-reduce.2.cloned.1.call-done = f32[512,512]{1,0:T(8,128)} async-done(((f32[512,512]{1,0:T(8,128)}), f32[512,512]{1,0:T(8,128)}) %all-reduce.2.cloned.1.call-update) | async-done | bytes 1048592 | tf_op jit(solution)/shard_map/psum | solution.py:24
  377.9 0.0 copy-done
  377.9 2.4 fusion.9
  380.2 0.3 fusion.10
  380.5 0.1 copy.12
  380.6 5.8 %cholesky.44 = f32[64,64]{1,0:T(8,128)S(1)} custom-call(f32[64,64]{1,0:T(8,128)S(1)} %fusion.5), custom_call_target="Cholesky" | custom-call | tf_op jit(solution)/shard_map/jit(cholesky)/cholesky | solution.py:11
  386.5 0.6 compare_reduce_fusion.1
  387.1 0.7 fusion
  387.8 4.9 %custom-call.6 = f32[1,64,64]{1,2,0:T(8,128)S(1)} custom-call(f32[1,64,64]{2,1,0:T(8,128)S(1)} %fusion), custom_call_target="InvertDiagBlocksLowerTriangular" | custom-call | tf_op jit(solution)/shard_map/triangular_solve/custom-call.0 | solution.py:12
  392.7 0.3 convolution_bitcast_fusion.2
  393.0 2.4 fusion.11
  395.4 0.3 fusion.12
  395.7 0.1 copy.13
  395.8 6.0 %cholesky.55 = f32[64,64]{1,0:T(8,128)S(1)} custom-call(f32[64,64]{1,0:T(8,128)S(1)} %fusion.3), custom_call_target="Cholesky" | custom-call | tf_op jit(solution)/shard_map/jit(cholesky)/cholesky | solution.py:11
  401.8 0.6 compare_reduce_fusion
  402.5 0.7 fusion.1
  403.1 4.9 %custom-call.7 = f32[1,64,64]{1,2,0:T(8,128)S(1)} custom-call(f32[1,64,64]{2,1,0:T(8,128)S(1)} %fusion.1), custom_call_target="InvertDiagBlocksLowerTriangular" | custom-call | tf_op jit(solution)/shard_map/triangular_solve/custom-call.0 | solution.py:12
  408.0 0.3 convolution_bitcast_fusion.1
  408.4 0.0 copy-start.2
  408.4 4.9 %convolution_bitcast_fusion = f32[64,1,1,2048]{3,0,2,1:T(8,128)S(1)} fusion(f32[512,64]{0,1:T(8,128)S(1)} %convolution_bitcast_fusion.1, f32[512,2048]{1,0:T(8,128)} %bitcast.44), kind=kOutput, calls=%fused_computation | convolution fusion | flops 805306368 | bytes 4849664 | tf_op jit(solution)/shard_map/dot_general | solution.py:29
  413.3 1.3 copy.14
  414.6 0.0 copy-done.2
  (4 shorter events, 0.1 us)
Async XLA Ops:
  7.2 370.7 %copy-start = (f32[512,64]{0,1:T(8,128)S(1)}, f32[512,64]{0,1:T(8,128)}, u32[]{:S(2)}) copy-start(f32[512,64]{0,1:T(8,128)} %param.6) | copy-start | bytes 393220
  7.2 370.7 %all-reduce.2.cloned.1.call-start = ((), (), s32[]{:S(2)}) async-start(), calls=%async_computation.1 | async-start | bytes 2097152 | tf_op jit(solution)/shard_map/psum | solution.py:24
  115.3 1.9 copy-start.1
  408.4 6.2 %copy-start.2 = (f32[512,64]{0,1:T(8,128)}, f32[512,64]{0,1:T(8,128)S(1)}, u32[]{:S(2)}) copy-start(f32[512,64]{0,1:T(8,128)S(1)} %convolution_bitcast_fusion.1) | copy-start | bytes 393220
Sparse Core Ops, SparseCore 0:
  125.3 252.5 all-reduce.1
where the time goes:
time: 422 us; the launch traced here: 421 us
  waiting for transfers between devices  253 us (60%)
  blocking collectives  103 us (24%)
  other arithmetic  24.4 us (6%)
  matrix products  18.7 us (4%)
  between operations  14.1 us (3%)
  local copies, waits for them, and re-layouts  8.07 us (2%)
    psum x1, waiting for transfers between devices, shards(): gram = lax.psum(local_gram, ('fibre', 'cols'))  253 us
    all_to_all x1, blocking collectives, shards(): lax.all_to_all(tensor, 'fibre', split_axis=2, concat_axis=0, tiled=True)  103 us
    another operation x6, other arithmetic, orthonormal(): lower = jnp.linalg.cholesky(squares)  13.2 us
    another operation x4, other arithmetic, orthonormal(): lax.linalg.triangular_solve(lower, product, left_side=False, lower=True,...  11.1 us
  transfers between devices with their start and end apart: 1, of which 1 were waited for; matrix products, arithmetic and copies ran while one was open for 0% of the time, Pallas kernels for 0%

commit v1 on v0

v1 whole, which is shorter than its diff:
```python
import jax
import jax.numpy as jnp
from jax import lax
from jax.experimental import pallas as pl
from jax.experimental.pallas import tpu as pltpu
from jax.sharding import PartitionSpec as P

MESH = pl.DeviceIdType.MESH
HIGHEST = lax.Precision.HIGHEST
F32 = jnp.float32

M = 512
RANK = 64
WIDTH = 2048
NZ = 8
ROWS = M // NZ
CHIPS = 16
CHUNKS = 8
CW = WIDTH // CHUNKS
HALF = M // 2
SLAB = HALF // CHIPS
LANES = 128
OFFSETS = (4, 3, 5, 2, 6, 1, 7)


def dot(a, b, contract):
    return lax.dot_general(
        a, b, (contract, ((), ())), precision=HIGHEST, preferred_element_type=F32
    )


def inverse_factor(squares):
    rows = lax.broadcasted_iota(jnp.int32, (RANK, LANES), 0)
    lanes = lax.broadcasted_iota(jnp.int32, (RANK, LANES), 1)
    start = jnp.where(lanes < RANK, squares, (lanes - RANK == rows).astype(F32))

    def panel(step, a):
        live = rows < RANK - 8 * step
        for t in range(8):
            scale = lax.rsqrt(a[t : t + 1, t : t + 1])
            row = a[t : t + 1, :] * scale
            column = a[:, t : t + 1] * scale
            update = jnp.where(live & (rows > t), a - column * row, a)
            a = jnp.where(rows == t, row, update)
        a = jnp.concatenate([a[8:], a[:8]], axis=0)
        return pltpu.roll(a, LANES - 8, 1)

    return lax.fori_loop(0, RANK // 8, panel, start)


def kernel(
    tensor,
    initial,
    slab_out,
    basis_out,
    stage,
    x,
    gram,
    core_in,
    half,
    plane_in,
    slab_g,
    z_y,
    z_g,
    own_y,
    y_all,
    own_w,
    w_all,
    load_sem,
    send_x,
    recv_x,
    send_p,
    recv_p,
    send_z,
    recv_z,
    send_c,
    recv_c,
):
    f, c = lax.axis_index("fibre"), lax.axis_index("cols")
    chip, core = c // 2, lax.rem(c, 2)
    chip_y, chip_x = chip // 4, lax.rem(chip, 4)
    other = 1 - core

    def z_at(offset):
        return lax.rem(f + offset, NZ)

    def chip_at(k):
        return lax.rem(chip_y + k // 4, 4) * 4 + lax.rem(chip_x + k % 4, 4)

    def send(src, dst, ssem, rsem, device):
        return pltpu.make_async_remote_copy(
            src_ref=src,
            dst_ref=dst,
            send_sem=ssem,
            recv_sem=rsem,
            device_id=device,
            device_id_type=MESH,
        )

    def load(j, g, to):
        columns = pl.ds(pl.multiple_of(j * CW, CW), CW)
        return pltpu.make_async_copy(
            tensor.at[:, 0, g, columns], to, load_sem.at[j, g]
        )

    def load_own(j):
        columns = pl.ds(pl.multiple_of(j * CW, CW), CW)
        return pltpu.make_async_copy(
            tensor.at[:, 0, f, columns], x.at[j, f], load_sem.at[j, NZ - 1]
        )

    @pl.loop(0, CHUNKS)
    def _(j):
        for i, offset in enumerate(OFFSETS):
            g = z_at(offset)
            pltpu.make_async_copy(
                tensor.at[:, 0, g, pl.ds(pl.multiple_of(j * CW, CW), CW)],
                stage.at[j, i],
                load_sem.at[j, i],
            ).start()
        load_own(j).start()

    barrier = pltpu.get_barrier_semaphore()
    for offset in OFFSETS:
        pl.semaphore_signal(
            barrier, inc=1, device_id=(z_at(offset), c), device_id_type=MESH
        )
    for k in range(1, CHIPS):
        pl.semaphore_signal(
            barrier, inc=1, device_id=(f, chip_at(k) * 2 + core), device_id_type=MESH
        )
    sibling = (f, chip * 2 + other)
    pl.semaphore_signal(barrier, inc=1, device_id=sibling, device_id_type=MESH)
    pl.semaphore_wait(barrier, NZ - 1 + CHIPS)

    def exchange(j, i):
        return send(
            stage.at[j, i],
            x.at[j, f],
            send_x.at[j, i],
            recv_x.at[j, i],
            (z_at(OFFSETS[i]), c),
        )

    @pl.loop(0, CHUNKS)
    def _(j):
        for i, offset in enumerate(OFFSETS):
            pltpu.make_async_copy(
                tensor.at[:, 0, z_at(offset), pl.ds(pl.multiple_of(j * CW, CW), CW)],
                stage.at[j, i],
                load_sem.at[j, i],
            ).wait()
            exchange(j, i).start()

    gram[...] = jnp.zeros_like(gram)

    @pl.loop(0, CHUNKS)
    def _(j):
        load_own(j).wait()
        for i in range(NZ - 1):
            exchange(j, i).wait_recv()
        block = x[j].reshape(M, CW)
        gram[...] += dot(block, block, ((1,), (1,)))

    mine = pl.ds(pl.multiple_of(core * HALF, HALF), HALF)
    theirs = pl.ds(pl.multiple_of(other * HALF, HALF), HALF)
    swap = send(gram.at[theirs], core_in, send_c.at[0], recv_c.at[0], sibling)
    swap.start()
    swap.wait_recv()
    half[...] = gram[mine] + core_in[...]

    def scatter(k):
        to = chip_at(k)
        return send(
            half.at[pl.ds(pl.multiple_of(to * SLAB, SLAB), SLAB)],
            plane_in.at[k],
            send_p.at[0, k],
            recv_p.at[0, k],
            (f, to * 2 + core),
        )

    for k in range(1, CHIPS):
        scatter(k).start()
    total = half[pl.ds(pl.multiple_of(chip * SLAB, SLAB), SLAB)]
    for k in range(1, CHIPS):
        scatter(k).wait_recv()
        total = total + plane_in[k]
    slab_g[...] = total

    start = initial[...]
    part = dot(total, start, ((1,), (1,)))
    own_y[0] = jnp.concatenate([part, jnp.zeros_like(part)], axis=1)

    def z_send_y(i):
        return send(
            own_y.at[0], z_y.at[i], send_z.at[0, i], recv_z.at[0, i], (z_at(OFFSETS[i]), c)
        )

    def z_send_g(i):
        return send(
            slab_g, z_g.at[i], send_z.at[1, i], recv_z.at[1, i], (z_at(OFFSETS[i]), c)
        )

    for i in range(NZ - 1):
        z_send_y(i).start()
    for i in range(NZ - 1):
        z_send_g(i).start()

    def z_sum(own, of):
        acc = None
        for z in range(NZ):
            value = own
            for i, offset in enumerate(OFFSETS):
                value = jnp.where(lax.rem(z + offset, NZ) == f, of[i], value)
            acc = value if acc is None else acc + value
        return acc

    for i in range(NZ - 1):
        z_send_y(i).wait_recv()
    own_y[1] = z_sum(own_y[0], z_y)

    def gather(own, whole, which):
        at = pl.ds(pl.multiple_of(chip * SLAB, SLAB), SLAB)
        whole[core, at] = own[...]

        def to_chip(k):
            return send(
                own,
                whole.at[core, at],
                send_p.at[1 + which, k],
                recv_p.at[1 + which, k],
                (f, chip_at(k) * 2 + core),
            )

        for k in range(1, CHIPS):
            to_chip(k).start()
        for k in range(1, CHIPS):
            to_chip(k).wait_recv()
        swap = send(
            whole.at[core], whole.at[core], send_c.at[1 + which], recv_c.at[1 + which], sibling
        )
        swap.start()
        sends.extend(to_chip(k) for k in range(1, CHIPS))
        sends.append(swap)
        return swap

    sends = [swap]
    gather(own_y.at[1], y_all, 0).wait_recv()
    y1 = y_all[...].reshape(M, LANES)

    for i in range(NZ - 1):
        z_send_g(i).wait_recv()
    own_g = z_sum(slab_g[...], z_g)
    own_w[...] = dot(own_g, y1, ((1,), (0,)))
    inverse1 = inverse_factor(dot(y1, y1, ((0,), (0,)))[:RANK])
    gather(own_w, w_all, 1).wait_recv()

    w = w_all[...].reshape(M, LANES)[:, :RANK]
    y2 = dot(w, inverse1[:, :RANK], ((1,), (1,)))
    squares = dot(y2, y2, ((0,), (0,)))
    inverse2 = inverse_factor(jnp.concatenate([squares, squares], axis=1))
    basis = dot(inverse2[:, :RANK], y2, ((1,), (1,)))
    basis_out[...] = basis

    for j in range(CHUNKS):
        slab_out[:, j * CW : (j + 1) * CW] = dot(
            basis, x[j].reshape(M, CW), ((1,), (0,))
        )

    @pl.loop(0, CHUNKS)
    def _(j):
        for i in range(NZ - 1):
            exchange(j, i).wait_send()

    for k in range(1, CHIPS):
        scatter(k).wait_send()
    for i in range(NZ - 1):
        z_send_y(i).wait_send()
        z_send_g(i).wait_send()
    for copy in sends:
        copy.wait_send()


def shards(tensor, initial):
    vmem = pl.BlockSpec(memory_space=pltpu.VMEM)
    slab, basis = pl.pallas_call(
        kernel,
        name="subspace",
        out_shape=(
            jax.ShapeDtypeStruct((RANK, WIDTH), F32),
            jax.ShapeDtypeStruct((RANK, M), F32),
        ),
        in_specs=[pl.BlockSpec(memory_space=pl.ANY), vmem],
        out_specs=(vmem, vmem),
        scratch_shapes=[
            pltpu.VMEM((CHUNKS, NZ - 1, ROWS, CW), F32),
            pltpu.VMEM((CHUNKS, NZ, ROWS, CW), F32),
            pltpu.VMEM((M, M), F32),
            pltpu.VMEM((HALF, M), F32),
            pltpu.VMEM((HALF, M), F32),
            pltpu.VMEM((CHIPS, SLAB, M), F32),
            pltpu.VMEM((SLAB, M), F32),
            pltpu.VMEM((NZ - 1, SLAB, LANES), F32),
            pltpu.VMEM((NZ - 1, SLAB, M), F32),
            pltpu.VMEM((2, SLAB, LANES), F32),
            pltpu.VMEM((2, HALF, LANES), F32),
            pltpu.VMEM((SLAB, LANES), F32),
            pltpu.VMEM((2, HALF, LANES), F32),
            pltpu.SemaphoreType.DMA((CHUNKS, NZ)),
            pltpu.SemaphoreType.DMA((CHUNKS, NZ - 1)),
            pltpu.SemaphoreType.DMA((CHUNKS, NZ - 1)),
            pltpu.SemaphoreType.DMA((3, CHIPS)),
            pltpu.SemaphoreType.DMA((3, CHIPS)),
            pltpu.SemaphoreType.DMA((2, NZ - 1)),
            pltpu.SemaphoreType.DMA((2, NZ - 1)),
            pltpu.SemaphoreType.DMA((3,)),
            pltpu.SemaphoreType.DMA((3,)),
        ],
        compiler_params=pltpu.CompilerParams(
            collective_id=0, has_side_effects=True, vmem_limit_bytes=56 * 1024 * 1024
        ),
    )(tensor, initial.T)
    return slab.reshape(RANK, 1, 1, WIDTH), basis.T


def solution(mesh):
    return jax.shard_map(
        shards,
        mesh=mesh,
        in_specs=(P("fibre", "cols", None, None), P()),
        out_specs=(P(None, "cols", "fibre", None), P()),
        check_vma=False,
    )
```

time: 422 us -> 158 us (0.37)
  waiting for transfers between devices: 253 us -> 0 us
  Pallas kernels: 0 us -> 153 us
  blocking collectives: 103 us -> 0 us
  other arithmetic: 24.4 us -> 0 us
  matrix products: 18.7 us -> 0 us
  between operations: 14.1 us -> 0.64 us
    psum x1 -> x0, waiting for transfers between devices: 253 us -> none  [shards(): gram = lax.psum(local_gram, ('fibre', 'cols'))]
    pallas_call x0 -> x1, Pallas kernels: none -> 153 us  [shards(): pl.pallas_call(kernel, name='subspace', out_shape=(jax.ShapeDtypeStruct((...]
    all_to_all x1 -> x0, blocking collectives: 103 us -> none  [shards(): lax.all_to_all(tensor, 'fibre', split_axis=2, concat_axis=0, tiled=True)]
    another operation x10 -> x0, other arithmetic: 24.3 us -> none  [the longest x6 13.2 us: orthonormal(): lower = jnp.linalg.cholesky(squares)]
    dot_general x6 -> x0, matrix products: 18 us -> none  [the longest x1 7.93 us: shards(): local_gram = jnp.dot(columns, columns.T, precision=highest)]
  transfers between devices with their start and end apart: 1 -> 0, of which waited for: 1 -> 0; matrix products, arithmetic and copies ran while one was open for 0% -> 0% of each run, Pallas kernels for 0% -> 0%
where the time goes in v1:
time: 158 us
  Pallas kernels  153 us (97%)
  local copies, waits for them, and re-layouts  3.94 us (2%)
    pallas_call x1, Pallas kernels, shards(): pl.pallas_call(kernel, name='subspace', out_shape=(jax.ShapeDtypeStruct((...  153 us
    unnamed x2, local copies, waits for them, and re-layouts  3.94 us

profile of v1, /device:TPU:1, one launch (start us, length us, event | category | flops | bytes accessed | tf_op | source)
XLA Modules:
  0.0 158.0 jit_solution(15389609972050901291)
XLA Ops:
  0.6 153.4 %subspace.1 = (f32[64,2048]{1,0:T(8,128)}, f32[64,512]{1,0:T(8,128)}) custom-call(f32[64,1,8,2048]{3,2,1,0:T(8,128)} %tensor.1, f32[64,512]{1,0:T(8,128)} %bitcast.4), custom_call_target="tpu_custom_call" | custom-call | tf_op jit(solution)/shard_map/subspace/pallas_call | solution.py:286
  154.0 2.4 %copy.4 = f32[64,1,1,2048]{3,2,1,0:T(1,128)} copy(f32[64,1,1,2048]{3,0,2,1:T(8,128)} %bitcast.3) | data formatting | bytes 1048576
  156.4 1.6 copy.6

commit v2 on v1

--- a/solution.py
+++ b/solution.py
@@ -29,10 +29,14 @@
     )
 
 
-def inverse_factor(squares):
+def augmented(squares):
     rows = lax.broadcasted_iota(jnp.int32, (RANK, LANES), 0)
     lanes = lax.broadcasted_iota(jnp.int32, (RANK, LANES), 1)
-    start = jnp.where(lanes < RANK, squares, (lanes - RANK == rows).astype(F32))
+    return jnp.where(lanes < RANK, squares, (lanes - RANK == rows).astype(F32))
+
+
+def eliminate(start, first, last):
+    rows = lax.broadcasted_iota(jnp.int32, (RANK, LANES), 0)
 
     def panel(step, a):
         live = rows < RANK - 8 * step
@@ -45,7 +49,7 @@
         a = jnp.concatenate([a[8:], a[:8]], axis=0)
         return pltpu.roll(a, LANES - 8, 1)
 
-    return lax.fori_loop(0, RANK // 8, panel, start)
+    return lax.fori_loop(first, last, panel, start)
 
 
 def kernel(
@@ -219,46 +223,50 @@
         z_send_y(i).wait_recv()
     own_y[1] = z_sum(own_y[0], z_y)
 
-    def gather(own, whole, which):
-        at = pl.ds(pl.multiple_of(chip * SLAB, SLAB), SLAB)
+    at = pl.ds(pl.multiple_of(chip * SLAB, SLAB), SLAB)
+
+    def to_chip(own, whole, which, k):
+        return send(
+            own,
+            whole.at[core, at],
+            send_p.at[which, k],
+            recv_p.at[which, k],
+            (f, chip_at(k) * 2 + core),
+        )
+
+    def to_core(whole, which):
+        return send(
+            whole.at[core], whole.at[core], send_c.at[which], recv_c.at[which], sibling
+        )
+
+    def gather_start(own, whole, which):
+        for k in range(1, CHIPS):
+            to_chip(own, whole, which, k).start()
         whole[core, at] = own[...]
 
-        def to_chip(k):
-            return send(
-                own,
-                whole.at[core, at],
-                send_p.at[1 + which, k],
-                recv_p.at[1 + which, k],
-                (f, chip_at(k) * 2 + core),
-            )
-
+    def gather_swap(own, whole, which):
         for k in range(1, CHIPS):
-            to_chip(k).start()
-        for k in range(1, CHIPS):
-            to_chip(k).wait_recv()
-        swap = send(
-            whole.at[core], whole.at[core], send_c.at[1 + which], recv_c.at[1 + which], sibling
-        )
-        swap.start()
-        sends.extend(to_chip(k) for k in range(1, CHIPS))
-        sends.append(swap)
-        return swap
-
-    sends = [swap]
-    gather(own_y.at[1], y_all, 0).wait_recv()
-    y1 = y_all[...].reshape(M, LANES)
-
+            to_chip(own, whole, which, k).wait_recv()
+        to_core(whole, which).start()
+
+    gather_start(own_y.at[1], y_all, 1)
+    gather_swap(own_y.at[1], y_all, 1)
     for i in range(NZ - 1):
         z_send_g(i).wait_recv()
     own_g = z_sum(slab_g[...], z_g)
+    to_core(y_all, 1).wait_recv()
+    y1 = y_all[...].reshape(M, LANES)
     own_w[...] = dot(own_g, y1, ((1,), (0,)))
-    inverse1 = inverse_factor(dot(y1, y1, ((0,), (0,)))[:RANK])
-    gather(own_w, w_all, 1).wait_recv()
+    gather_start(own_w, w_all, 2)
+    partial = eliminate(augmented(dot(y1, y1, ((0,), (0,)))[:RANK]), 0, 6)
+    gather_swap(own_w, w_all, 2)
+    inverse1 = eliminate(partial, 6, 8)
+    to_core(w_all, 2).wait_recv()
 
     w = w_all[...].reshape(M, LANES)[:, :RANK]
     y2 = dot(w, inverse1[:, :RANK], ((1,), (1,)))
     squares = dot(y2, y2, ((0,), (0,)))
-    inverse2 = inverse_factor(jnp.concatenate([squares, squares], axis=1))
+    inverse2 = eliminate(augmented(jnp.concatenate([squares, squares], axis=1)), 0, 8)
     basis = dot(inverse2[:, :RANK], y2, ((1,), (1,)))
     basis_out[...] = basis
 
@@ -277,8 +285,12 @@
     for i in range(NZ - 1):
         z_send_y(i).wait_send()
         z_send_g(i).wait_send()
-    for copy in sends:
-        copy.wait_send()
+    for k in range(1, CHIPS):
+        to_chip(own_y.at[1], y_all, 1, k).wait_send()
+        to_chip(own_w, w_all, 2, k).wait_send()
+    swap.wait_send()
+    to_core(y_all, 1).wait_send()
+    to_core(w_all, 2).wait_send()
 
 
 def shards(tensor, initial):
@@ -317,7 +329,7 @@
             pltpu.SemaphoreType.DMA((3,)),
         ],
         compiler_params=pltpu.CompilerParams(
-            collective_id=0, has_side_effects=True, vmem_limit_bytes=56 * 1024 * 1024
+            collective_id=0, has_side_effects=True, vmem_limit_bytes=51 * 1024 * 1024
         ),
     )(tensor, initial.T)
     return slab.reshape(RANK, 1, 1, WIDTH), basis.T

time: 158 us -> 150 us (0.949)
  Pallas kernels: 153 us -> 146 us
    pallas_call x1, Pallas kernels: 153 us -> 146 us  [shards(): pl.pallas_call(kernel, name='subspace', out_shape=(jax.ShapeDtypeStruct((...]
    unnamed x2 -> x4, local copies, waits for them, and re-layouts: 3.94 us -> 2.89 us
where the time goes in v2:
time: 150 us
  Pallas kernels  146 us (97%)
  local copies, waits for them, and re-layouts  2.89 us (2%)
    pallas_call x1, Pallas kernels, shards(): pl.pallas_call(kernel, name='subspace', out_shape=(jax.ShapeDtypeStruct((...  146 us

profile of v2, /device:TPU:1, one launch (start us, length us, event | category | flops | bytes accessed | tf_op | source)
XLA Modules:
  0.0 149.9 jit_solution(4719100823982259647)
XLA Ops:
  0.6 0.0 copy-start
  0.6 0.9 copy-done
  1.5 146.4 %subspace.1 = (f32[64,2048]{1,0:T(8,128)S(1)}, f32[64,512]{1,0:T(8,128)S(1)}) custom-call(f32[64,1,8,2048]{3,2,1,0:T(8,128)} %tensor.1, f32[64,512]{1,0:T(8,128)S(1)} %bitcast.4), custom_call_target="tpu_custom_call" | custom-call | tf_op jit(solution)/shard_map/subspace/pallas_call | solution.py:298
  147.9 1.3 copy.4
  149.3 0.7 copy.6
Async XLA Ops:
  0.6 0.9 copy-start

commit v3 on v1

v3 whole, which is shorter than its diff:
```python
import jax
import jax.numpy as jnp
from jax import lax
from jax.experimental import pallas as pl
from jax.experimental.pallas import tpu as pltpu
from jax.sharding import PartitionSpec as P

MESH = pl.DeviceIdType.MESH
HIGHEST = lax.Precision.HIGHEST
F32 = jnp.float32

M = 512
RANK = 64
WIDTH = 2048
NZ = 8
ROWS = M // NZ
CHIPS = 16
CHUNKS = 16
CW = WIDTH // CHUNKS
HALF = M // 2
SLAB = HALF // CHIPS
LANES = 128
OFFSETS = (4, 3, 5, 2, 6, 1, 7)


def dot(a, b, contract):
    return lax.dot_general(
        a, b, (contract, ((), ())), precision=HIGHEST, preferred_element_type=F32
    )


def augmented(squares):
    rows = lax.broadcasted_iota(jnp.int32, (RANK, LANES), 0)
    lanes = lax.broadcasted_iota(jnp.int32, (RANK, LANES), 1)
    return jnp.where(lanes < RANK, squares, (lanes - RANK == rows).astype(F32))


def inverse_factor(squares):
    rows = lax.broadcasted_iota(jnp.int32, (RANK, LANES), 0)
    top = lax.broadcasted_iota(jnp.int32, (8, LANES), 0)

    def panel(step, a):
        live = rows < RANK - 8 * step
        columns = [
            jnp.where(live, jnp.broadcast_to(a[:, t : t + 1], (RANK, LANES)), 0.0)
            for t in range(8)
        ]
        for t in range(8):
            pivot = columns[t][t : t + 1]
            inverse = 1.0 / pivot
            column = jnp.where(rows > t, columns[t], 0.0)
            row = a[t : t + 1]
            for q in range(t + 1, 8):
                columns[q] = columns[q] - column * (columns[q][t : t + 1] * inverse)
            a = a - column * (row * inverse)
            head = jnp.where(top == t, row * lax.rsqrt(pivot), a[:8])
            a = jnp.concatenate([head, a[8:]], axis=0)
        a = jnp.concatenate([a[8:], a[:8]], axis=0)
        return pltpu.roll(a, LANES - 8, 1)

    return lax.fori_loop(0, RANK // 8, panel, augmented(squares))[:, :RANK]


def pack(y):
    y = y.reshape(y.shape[0] // 16, 2, 8, RANK)
    return jnp.concatenate([y[:, 0], y[:, 1]], axis=2)


def unpack(y):
    n = y.shape[0]
    y = jnp.stack([y[:, :, :RANK], y[:, :, RANK:]], axis=1)
    return y.reshape(16 * n, RANK)


def kernel(
    tensor,
    initial,
    slab_out,
    basis_out,
    x,
    gram,
    core_g,
    half_g,
    plane_g,
    slab_g,
    z_g,
    part_y,
    core_y,
    half_y,
    plane_y,
    z_y,
    own_y,
    y_all,
    w_all,
    load_sem,
    send_x,
    recv_x,
    send_p,
    recv_p,
    send_z,
    recv_z,
    send_c,
    recv_c,
):
    f, c = lax.axis_index("fibre"), lax.axis_index("cols")
    chip, core = c // 2, lax.rem(c, 2)
    chip_y, chip_x = chip // 4, lax.rem(chip, 4)
    other = 1 - core
    sibling = (f, chip * 2 + other)

    def z_at(offset):
        return lax.rem(f + offset, NZ)

    def chip_at(k):
        return lax.rem(chip_y + k // 4, 4) * 4 + lax.rem(chip_x + k % 4, 4)

    def send(src, dst, ssem, rsem, device):
        return pltpu.make_async_remote_copy(
            src_ref=src,
            dst_ref=dst,
            send_sem=ssem,
            recv_sem=rsem,
            device_id=device,
            device_id_type=MESH,
        )

    def piece(j, z):
        return tensor.at[:, 0, z, pl.ds(pl.multiple_of(j * CW, CW), CW)]

    def load_own(j):
        return pltpu.make_async_copy(piece(j, f), x.at[j, f], load_sem.at[j])

    def exchange(j, i):
        to = z_at(OFFSETS[i])
        return send(
            piece(j, to), x.at[j, f], send_x.at[j, i], recv_x.at[j, i], (to, c)
        )

    def to_core(src, dst, which):
        return send(src, dst, send_c.at[which], recv_c.at[which], sibling)

    def to_chip(src, dst, which, k):
        return send(
            src,
            dst,
            send_p.at[which, k],
            recv_p.at[which, k],
            (f, chip_at(k) * 2 + core),
        )

    def to_z(src, dst, which, i):
        return send(
            src, dst, send_z.at[which, i], recv_z.at[which, i], (z_at(OFFSETS[i]), c)
        )

    def each(count, start, make, act):
        for k in range(start, count):
            act(make(k))

    def started(copy):
        copy.start()

    def arrived(copy):
        copy.wait_recv()

    def left(copy):
        copy.wait_send()

    barrier = pltpu.get_barrier_semaphore()
    for offset in OFFSETS:
        pl.semaphore_signal(
            barrier, inc=1, device_id=(z_at(offset), c), device_id_type=MESH
        )
    for k in range(1, CHIPS):
        pl.semaphore_signal(
            barrier, inc=1, device_id=(f, chip_at(k) * 2 + core), device_id_type=MESH
        )
    pl.semaphore_signal(barrier, inc=1, device_id=sibling, device_id_type=MESH)

    @pl.loop(0, CHUNKS)
    def _(j):
        load_own(j).start()

    gram[...] = jnp.zeros_like(gram)
    pl.semaphore_wait(barrier, NZ - 1 + CHIPS)

    @pl.loop(0, CHUNKS)
    def _(j):
        for i in range(NZ - 1):
            exchange(j, i).start()

    start = initial[...]

    def chunk_arrived(j):
        load_own(j).wait()
        for i in range(NZ - 1):
            exchange(j, i).wait_recv()

    @pl.loop(0, CHUNKS - 1)
    def _(j):
        chunk_arrived(j)
        block = x[j].reshape(M, CW)
        gram[...] += dot(block, block, ((1,), (1,)))

    early = dot(gram[...], start, ((1,), (1,)))
    chunk_arrived(CHUNKS - 1)
    block = x[CHUNKS - 1].reshape(M, CW)
    late = dot(block, dot(start, block, ((1,), (0,))), ((1,), (1,)))
    part_y[...] = pack(early + late).reshape(2, CHIPS, 8, LANES)

    swap_y = to_core(part_y.at[other], core_y, 0)
    swap_y.start()
    gram[...] += dot(block, block, ((1,), (1,)))
    mine = pl.ds(pl.multiple_of(core * HALF, HALF), HALF)
    theirs = pl.ds(pl.multiple_of(other * HALF, HALF), HALF)
    swap_g = to_core(gram.at[theirs], core_g, 1)
    swap_g.start()

    swap_y.wait_recv()
    half_y[...] = part_y[core] + core_y[...]

    def scatter_y(k):
        return to_chip(half_y.at[chip_at(k)], plane_y.at[k], 0, k)

    each(CHIPS, 1, scatter_y, started)

    swap_g.wait_recv()
    half_g[...] = gram[mine] + core_g[...]

    def scatter_g(k):
        rows = pl.ds(pl.multiple_of(chip_at(k) * SLAB, SLAB), SLAB)
        return to_chip(half_g.at[rows], plane_g.at[k], 1, k)

    each(CHIPS, 1, scatter_g, started)

    each(CHIPS, 1, scatter_y, arrived)
    total = half_y[chip]
    for k in range(1, CHIPS):
        total = total + plane_y[k]
    own_y[0] = total

    def z_send_y(i):
        return to_z(own_y.at[0], z_y.at[i], 0, i)

    each(NZ - 1, 0, z_send_y, started)

    def z_sum(own, of):
        acc = None
        for z in range(NZ):
            value = own
            for i, offset in enumerate(OFFSETS):
                value = jnp.where(lax.rem(z + offset, NZ) == f, of[i], value)
            acc = value if acc is None else acc + value
        return acc

    each(NZ - 1, 0, z_send_y, arrived)
    own_y[1] = z_sum(own_y[0], z_y)

    def gather_y(k):
        return to_chip(own_y.at[1], y_all.at[core, chip], 2, k)

    def gather_w(k):
        return to_chip(own_y.at[2], w_all.at[core, chip], 3, k)

    each(CHIPS, 1, gather_y, started)
    y_all[core, chip] = own_y[1]

    each(CHIPS, 1, scatter_g, arrived)
    total = half_g[pl.ds(pl.multiple_of(chip * SLAB, SLAB), SLAB)]
    for k in range(1, CHIPS):
        total = total + plane_g[k]
    slab_g[...] = total

    def z_send_g(i):
        return to_z(slab_g, z_g.at[i], 1, i)

    each(NZ - 1, 0, z_send_g, started)

    each(CHIPS, 1, gather_y, arrived)
    join_y = to_core(y_all.at[core], y_all.at[core], 2)
    join_y.start()
    join_y.wait_recv()
    y1 = unpack(y_all[...].reshape(2 * CHIPS, 8, LANES))
    squares = dot(y1, y1, ((0,), (0,)))
    inverse1 = inverse_factor(jnp.concatenate([squares, squares], axis=1))

    each(NZ - 1, 0, z_send_g, arrived)
    own_g = z_sum(slab_g[...], z_g)
    own_y[2] = pack(dot(own_g, y1, ((1,), (0,))))[0]
    each(CHIPS, 1, gather_w, started)
    w_all[core, chip] = own_y[2]
    each(CHIPS, 1, gather_w, arrived)
    join_w = to_core(w_all.at[core], w_all.at[core], 3)
    join_w.start()
    join_w.wait_recv()

    w = unpack(w_all[...].reshape(2 * CHIPS, 8, LANES))
    y2 = dot(inverse1, w, ((1,), (1,)))
    squares = dot(y2, y2, ((1,), (1,)))
    inverse2 = inverse_factor(jnp.concatenate([squares, squares], axis=1))
    basis = dot(inverse2, y2, ((1,), (0,)))
    basis_out[...] = basis

    for j in range(0, CHUNKS, 2):
        pair = jnp.concatenate([x[j].reshape(M, CW), x[j + 1].reshape(M, CW)], axis=1)
        slab_out[:, j * CW : (j + 2) * CW] = dot(basis, pair, ((1,), (0,)))

    @pl.loop(0, CHUNKS)
    def _(j):
        for i in range(NZ - 1):
            exchange(j, i).wait_send()

    for make in (scatter_y, scatter_g, gather_y, gather_w):
        each(CHIPS, 1, make, left)
    for make in (z_send_y, z_send_g):
        each(NZ - 1, 0, make, left)
    for copy in (swap_y, swap_g, join_y, join_w):
        copy.wait_send()


def shards(tensor, initial):
    vmem = pl.BlockSpec(memory_space=pltpu.VMEM)
    slab, basis = pl.pallas_call(
        kernel,
        name="subspace",
        out_shape=(
            jax.ShapeDtypeStruct((RANK, WIDTH), F32),
            jax.ShapeDtypeStruct((RANK, M), F32),
        ),
        in_specs=[pl.BlockSpec(memory_space=pl.ANY), vmem],
        out_specs=(vmem, vmem),
        scratch_shapes=[
            pltpu.VMEM((CHUNKS, NZ, ROWS, CW), F32),
            pltpu.VMEM((M, M), F32),
            pltpu.VMEM((HALF, M), F32),
            pltpu.VMEM((HALF, M), F32),
            pltpu.VMEM((CHIPS, SLAB, M), F32),
            pltpu.VMEM((SLAB, M), F32),
            pltpu.VMEM((NZ - 1, SLAB, M), F32),
            pltpu.VMEM((2, CHIPS, 8, LANES), F32),
            pltpu.VMEM((CHIPS, 8, LANES), F32),
            pltpu.VMEM((CHIPS, 8, LANES), F32),
            pltpu.VMEM((CHIPS, 8, LANES), F32),
            pltpu.VMEM((NZ - 1, 8, LANES), F32),
            pltpu.VMEM((3, 8, LANES), F32),
            pltpu.VMEM((2, CHIPS, 8, LANES), F32),
            pltpu.VMEM((2, CHIPS, 8, LANES), F32),
            pltpu.SemaphoreType.DMA((CHUNKS,)),
            pltpu.SemaphoreType.DMA((CHUNKS, NZ - 1)),
            pltpu.SemaphoreType.DMA((CHUNKS, NZ - 1)),
            pltpu.SemaphoreType.DMA((4, CHIPS)),
            pltpu.SemaphoreType.DMA((4, CHIPS)),
            pltpu.SemaphoreType.DMA((2, NZ - 1)),
            pltpu.SemaphoreType.DMA((2, NZ - 1)),
            pltpu.SemaphoreType.DMA((4,)),
            pltpu.SemaphoreType.DMA((4,)),
        ],
        compiler_params=pltpu.CompilerParams(
            collective_id=0, has_side_effects=True, vmem_limit_bytes=51 * 1024 * 1024
        ),
    )(tensor, initial.T)
    return slab.reshape(RANK, 1, 1, WIDTH), basis.T


def solution(mesh):
    return jax.shard_map(
        shards,
        mesh=mesh,
        in_specs=(P("fibre", "cols", None, None), P()),
        out_specs=(P(None, "cols", "fibre", None), P()),
        check_vma=False,
    )
```

time: 158 us -> 143 us (0.905)
  Pallas kernels: 153 us -> 140 us
    pallas_call x1, Pallas kernels: 153 us -> 140 us  [shards(): pl.pallas_call(kernel, name='subspace', out_shape=(jax.ShapeDtypeStruct((...]
    unnamed x2 -> x4, local copies, waits for them, and re-layouts: 3.94 us -> 2.89 us
where the time goes in v3:
time: 143 us
  Pallas kernels  140 us (98%)
  local copies, waits for them, and re-layouts  2.89 us (2%)
    pallas_call x1, Pallas kernels, shards(): pl.pallas_call(kernel, name='subspace', out_shape=(jax.ShapeDtypeStruct((...  140 us
    unnamed x4, local copies, waits for them, and re-layouts  2.89 us

profile of v3, /device:TPU:1, one launch (start us, length us, event | category | flops | bytes accessed | tf_op | source)
XLA Modules:
  0.0 143.1 jit_solution(14200416376871349990)
XLA Ops:
  0.6 0.0 copy-start
  0.6 0.9 copy-done
  1.5 139.6 %subspace.1 = (f32[64,2048]{1,0:T(8,128)S(1)}, f32[64,512]{1,0:T(8,128)S(1)}) custom-call(f32[64,1,8,2048]{3,2,1,0:T(8,128)} %tensor.1, f32[64,512]{1,0:T(8,128)S(1)} %bitcast.4), custom_call_target="tpu_custom_call" | custom-call | tf_op jit(solution)/shard_map/subspace/pallas_call | solution.py:323
  141.1 1.3 copy.4
  142.4 0.7 copy.6
Async XLA Ops:
  0.6 0.9 copy-start

commit v4 on v3

--- a/solution.py
+++ b/solution.py
@@ -21,6 +21,14 @@
 SLAB = HALF // CHIPS
 LANES = 128
 OFFSETS = (4, 3, 5, 2, 6, 1, 7)
+
+
+def hops(k):
+    return min(k // 4, 4 - k // 4) + min(k % 4, 4 - k % 4)
+
+
+NEXT = tuple(sorted(range(1, CHIPS), key=hops, reverse=True))
+PEERS = tuple((k, o) for k in NEXT for o in (0, 1)) + ((0, 1),)
 
 
 def dot(a, b, contract):
@@ -85,8 +93,6 @@
     slab_g,
     z_g,
     part_y,
-    core_y,
-    half_y,
     plane_y,
     z_y,
     own_y,
@@ -97,6 +103,8 @@
     recv_x,
     send_p,
     recv_p,
+    send_d,
+    recv_d,
     send_z,
     recv_z,
     send_c,
@@ -136,16 +144,19 @@
             piece(j, to), x.at[j, f], send_x.at[j, i], recv_x.at[j, i], (to, c)
         )
 
-    def to_core(src, dst, which):
-        return send(src, dst, send_c.at[which], recv_c.at[which], sibling)
-
-    def to_chip(src, dst, which, k):
+    def to_chip(src, dst, k):
         return send(
-            src,
-            dst,
-            send_p.at[which, k],
-            recv_p.at[which, k],
-            (f, chip_at(k) * 2 + core),
+            src, dst, send_p.at[k], recv_p.at[k], (f, chip_at(k) * 2 + core)
+        )
+
+    def peer(n):
+        k, o = PEERS[n]
+        return chip_at(k), other if o else core
+
+    def to_peer(src, dst, which, n):
+        to, at = peer(n)
+        return send(
+            src, dst, send_d.at[which, n], recv_d.at[which, n], (f, to * 2 + at)
         )
 
     def to_z(src, dst, which, i):
@@ -153,8 +164,8 @@
             src, dst, send_z.at[which, i], recv_z.at[which, i], (z_at(OFFSETS[i]), c)
         )
 
-    def each(count, start, make, act):
-        for k in range(start, count):
+    def each(order, make, act):
+        for k in order:
             act(make(k))
 
     def started(copy):
@@ -171,78 +182,79 @@
         pl.semaphore_signal(
             barrier, inc=1, device_id=(z_at(offset), c), device_id_type=MESH
         )
-    for k in range(1, CHIPS):
+    for n in range(len(PEERS)):
+        to, at = peer(n)
         pl.semaphore_signal(
-            barrier, inc=1, device_id=(f, chip_at(k) * 2 + core), device_id_type=MESH
-        )
-    pl.semaphore_signal(barrier, inc=1, device_id=sibling, device_id_type=MESH)
+            barrier, inc=1, device_id=(f, to * 2 + at), device_id_type=MESH
+        )
 
     @pl.loop(0, CHUNKS)
     def _(j):
         load_own(j).start()
 
     gram[...] = jnp.zeros_like(gram)
-    pl.semaphore_wait(barrier, NZ - 1 + CHIPS)
+    pl.semaphore_wait(barrier, NZ - 1 + len(PEERS))
 
     @pl.loop(0, CHUNKS)
     def _(j):
         for i in range(NZ - 1):
             exchange(j, i).start()
 
-    start = initial[...]
-
-    def chunk_arrived(j):
+    @pl.loop(0, CHUNKS)
+    def _(j):
         load_own(j).wait()
         for i in range(NZ - 1):
             exchange(j, i).wait_recv()
-
-    @pl.loop(0, CHUNKS - 1)
-    def _(j):
-        chunk_arrived(j)
         block = x[j].reshape(M, CW)
         gram[...] += dot(block, block, ((1,), (1,)))
 
-    early = dot(gram[...], start, ((1,), (1,)))
-    chunk_arrived(CHUNKS - 1)
-    block = x[CHUNKS - 1].reshape(M, CW)
-    late = dot(block, dot(start, block, ((1,), (0,))), ((1,), (1,)))
-    part_y[...] = pack(early + late).reshape(2, CHIPS, 8, LANES)
-
-    swap_y = to_core(part_y.at[other], core_y, 0)
-    swap_y.start()
-    gram[...] += dot(block, block, ((1,), (1,)))
+    zs, peers = range(NZ - 1), range(len(PEERS))
+
     mine = pl.ds(pl.multiple_of(core * HALF, HALF), HALF)
     theirs = pl.ds(pl.multiple_of(other * HALF, HALF), HALF)
-    swap_g = to_core(gram.at[theirs], core_g, 1)
+    swap_g = send(gram.at[theirs], core_g, send_c.at[0], recv_c.at[0], sibling)
     swap_g.start()
 
-    swap_y.wait_recv()
-    half_y[...] = part_y[core] + core_y[...]
-
-    def scatter_y(k):
-        return to_chip(half_y.at[chip_at(k)], plane_y.at[k], 0, k)
-
-    each(CHIPS, 1, scatter_y, started)
+    part_y[...] = pack(dot(gram[...], initial[...], ((1,), (1,)))).reshape(
+        2, CHIPS, 8, LANES
+    )
+
+    def scatter_y(n):
+        to, at = peer(n)
+        return to_peer(part_y.at[at, to], plane_y.at[n], 0, n)
+
+    each(peers, scatter_y, started)
 
     swap_g.wait_recv()
     half_g[...] = gram[mine] + core_g[...]
 
     def scatter_g(k):
         rows = pl.ds(pl.multiple_of(chip_at(k) * SLAB, SLAB), SLAB)
-        return to_chip(half_g.at[rows], plane_g.at[k], 1, k)
-
-    each(CHIPS, 1, scatter_g, started)
-
-    each(CHIPS, 1, scatter_y, arrived)
-    total = half_y[chip]
-    for k in range(1, CHIPS):
-        total = total + plane_y[k]
+        return to_chip(half_g.at[rows], plane_g.at[k], k)
+
+    each(NEXT, scatter_g, started)
+
+    each(peers, scatter_y, arrived)
+    total = part_y[core, chip]
+    for n in peers:
+        total = total + plane_y[n]
     own_y[0] = total
 
     def z_send_y(i):
         return to_z(own_y.at[0], z_y.at[i], 0, i)
 
-    each(NZ - 1, 0, z_send_y, started)
+    each(zs, z_send_y, started)
+
+    each(NEXT, scatter_g, arrived)
+    total = half_g[pl.ds(pl.multiple_of(chip * SLAB, SLAB), SLAB)]
+    for k in NEXT:
+        total = total + plane_g[k]
+    slab_g[...] = total
+
+    def z_send_g(i):
+        return to_z(slab_g, z_g.at[i], 1, i)
+
+    each(zs, z_send_g, started)
 
     def z_sum(own, of):
         acc = None
@@ -253,46 +265,28 @@
             acc = value if acc is None else acc + value
         return acc
 
-    each(NZ - 1, 0, z_send_y, arrived)
+    each(zs, z_send_y, arrived)
     own_y[1] = z_sum(own_y[0], z_y)
 
-    def gather_y(k):
-        return to_chip(own_y.at[1], y_all.at[core, chip], 2, k)
-
-    def gather_w(k):
-        return to_chip(own_y.at[2], w_all.at[core, chip], 3, k)
-
-    each(CHIPS, 1, gather_y, started)
+    def gather_y(n):
+        return to_peer(own_y.at[1], y_all.at[core, chip], 1, n)
+
+    def gather_w(n):
+        return to_peer(own_y.at[2], w_all.at[core, chip], 2, n)
+
+    each(peers, gather_y, started)
     y_all[core, chip] = own_y[1]
-
-    each(CHIPS, 1, scatter_g, arrived)
-    total = half_g[pl.ds(pl.multiple_of(chip * SLAB, SLAB), SLAB)]
-    for k in range(1, CHIPS):
-        total = total + plane_g[k]
-    slab_g[...] = total
-
-    def z_send_g(i):
-        return to_z(slab_g, z_g.at[i], 1, i)
-
-    each(NZ - 1, 0, z_send_g, started)
-
-    each(CHIPS, 1, gather_y, arrived)
-    join_y = to_core(y_all.at[core], y_all.at[core], 2)
-    join_y.start()
-    join_y.wait_recv()
+    each(peers, gather_y, arrived)
     y1 = unpack(y_all[...].reshape(2 * CHIPS, 8, LANES))
+
+    each(zs, z_send_g, arrived)
+    own_g = z_sum(slab_g[...], z_g)
+    own_y[2] = pack(dot(own_g, y1, ((1,), (0,))))[0]
+    each(peers, gather_w, started)
+    w_all[core, chip] = own_y[2]
     squares = dot(y1, y1, ((0,), (0,)))
     inverse1 = inverse_factor(jnp.concatenate([squares, squares], axis=1))
-
-    each(NZ - 1, 0, z_send_g, arrived)
-    own_g = z_sum(slab_g[...], z_g)
-    own_y[2] = pack(dot(own_g, y1, ((1,), (0,))))[0]
-    each(CHIPS, 1, gather_w, started)
-    w_all[core, chip] = own_y[2]
-    each(CHIPS, 1, gather_w, arrived)
-    join_w = to_core(w_all.at[core], w_all.at[core], 3)
-    join_w.start()
-    join_w.wait_recv()
+    each(peers, gather_w, arrived)
 
     w = unpack(w_all[...].reshape(2 * CHIPS, 8, LANES))
     y2 = dot(inverse1, w, ((1,), (1,)))
@@ -310,12 +304,12 @@
         for i in range(NZ - 1):
             exchange(j, i).wait_send()
 
-    for make in (scatter_y, scatter_g, gather_y, gather_w):
-        each(CHIPS, 1, make, left)
+    for make in (scatter_y, gather_y, gather_w):
+        each(peers, make, left)
     for make in (z_send_y, z_send_g):
-        each(NZ - 1, 0, make, left)
-    for copy in (swap_y, swap_g, join_y, join_w):
-        copy.wait_send()
+        each(zs, make, left)
+    each(NEXT, scatter_g, left)
+    swap_g.wait_send()
 
 
 def shards(tensor, initial):
@@ -338,9 +332,7 @@
             pltpu.VMEM((SLAB, M), F32),
             pltpu.VMEM((NZ - 1, SLAB, M), F32),
             pltpu.VMEM((2, CHIPS, 8, LANES), F32),
-            pltpu.VMEM((CHIPS, 8, LANES), F32),
-            pltpu.VMEM((CHIPS, 8, LANES), F32),
-            pltpu.VMEM((CHIPS, 8, LANES), F32),
+            pltpu.VMEM((len(PEERS), 8, LANES), F32),
             pltpu.VMEM((NZ - 1, 8, LANES), F32),
             pltpu.VMEM((3, 8, LANES), F32),
             pltpu.VMEM((2, CHIPS, 8, LANES), F32),
@@ -348,12 +340,14 @@
             pltpu.SemaphoreType.DMA((CHUNKS,)),
             pltpu.SemaphoreType.DMA((CHUNKS, NZ - 1)),
             pltpu.SemaphoreType.DMA((CHUNKS, NZ - 1)),
-            pltpu.SemaphoreType.DMA((4, CHIPS)),
-            pltpu.SemaphoreType.DMA((4, CHIPS)),
+            pltpu.SemaphoreType.DMA((CHIPS,)),
+            pltpu.SemaphoreType.DMA((CHIPS,)),
+            pltpu.SemaphoreType.DMA((3, len(PEERS))),
+            pltpu.SemaphoreType.DMA((3, len(PEERS))),
             pltpu.SemaphoreType.DMA((2, NZ - 1)),
             pltpu.SemaphoreType.DMA((2, NZ - 1)),
-            pltpu.SemaphoreType.DMA((4,)),
-            pltpu.SemaphoreType.DMA((4,)),
+            pltpu.SemaphoreType.DMA((1,)),
+            pltpu.SemaphoreType.DMA((1,)),
         ],
         compiler_params=pltpu.CompilerParams(
             collective_id=0, has_side_effects=True, vmem_limit_bytes=51 * 1024 * 1024

time: 143 us -> 141 us (0.986)
  Pallas kernels: 140 us -> 138 us
    pallas_call x1, Pallas kernels: 140 us -> 138 us  [shards(): pl.pallas_call(kernel, name='subspace', out_shape=(jax.ShapeDtypeStruct((...]
where the time goes in v4:
time: 141 us
  Pallas kernels  138 us (98%)
  local copies, waits for them, and re-layouts  2.89 us (2%)
    pallas_call x1, Pallas kernels, shards(): pl.pallas_call(kernel, name='subspace', out_shape=(jax.ShapeDtypeStruct((...  138 us
    unnamed x4, local copies, waits for them, and re-layouts  2.89 us

profile of v4, /device:TPU:1, one launch (start us, length us, event | category | flops | bytes accessed | tf_op | source)
XLA Modules:
  0.0 141.4 jit_solution(13235001518124294006)
XLA Ops:
  0.6 0.0 copy-start
  0.6 0.9 copy-done
  1.5 137.8 %subspace.1 = (f32[64,2048]{1,0:T(8,128)S(1)}, f32[64,512]{1,0:T(8,128)S(1)}) custom-call(f32[64,1,8,2048]{3,2,1,0:T(8,128)} %tensor.1, f32[64,512]{1,0:T(8,128)S(1)} %bitcast.4), custom_call_target="tpu_custom_call" | custom-call | tf_op jit(solution)/shard_map/subspace/pallas_call | solution.py:317
  139.4 1.3 copy.4
  140.7 0.7 copy.6
Async XLA Ops:
  0.6 0.9 copy-start

commit v5 on v4

--- a/solution.py
+++ b/solution.py
@@ -19,6 +19,7 @@
 CW = WIDTH // CHUNKS
 HALF = M // 2
 SLAB = HALF // CHIPS
+SIDES = 2
 LANES = 128
 OFFSETS = (4, 3, 5, 2, 6, 1, 7)
 
@@ -144,11 +145,6 @@
             piece(j, to), x.at[j, f], send_x.at[j, i], recv_x.at[j, i], (to, c)
         )
 
-    def to_chip(src, dst, k):
-        return send(
-            src, dst, send_p.at[k], recv_p.at[k], (f, chip_at(k) * 2 + core)
-        )
-
     def peer(n):
         k, o = PEERS[n]
         return chip_at(k), other if o else core
@@ -212,8 +208,18 @@
 
     mine = pl.ds(pl.multiple_of(core * HALF, HALF), HALF)
     theirs = pl.ds(pl.multiple_of(other * HALF, HALF), HALF)
-    swap_g = send(gram.at[theirs], core_g, send_c.at[0], recv_c.at[0], sibling)
-    swap_g.start()
+    sides = tuple(pl.ds(h * M // SIDES, M // SIDES) for h in range(SIDES))
+
+    def swap_g(h):
+        return send(
+            gram.at[theirs, sides[h]],
+            core_g.at[:, sides[h]],
+            send_c.at[h],
+            recv_c.at[h],
+            sibling,
+        )
+
+    each(range(SIDES), swap_g, started)
 
     part_y[...] = pack(dot(gram[...], initial[...], ((1,), (1,)))).reshape(
         2, CHIPS, 8, LANES
@@ -225,14 +231,21 @@
 
     each(peers, scatter_y, started)
 
-    swap_g.wait_recv()
-    half_g[...] = gram[mine] + core_g[...]
-
-    def scatter_g(k):
+    def scatter_g(h, k):
         rows = pl.ds(pl.multiple_of(chip_at(k) * SLAB, SLAB), SLAB)
-        return to_chip(half_g.at[rows], plane_g.at[k], k)
-
-    each(NEXT, scatter_g, started)
+        return send(
+            half_g.at[rows, sides[h]],
+            plane_g.at[k, :, sides[h]],
+            send_p.at[h, k],
+            recv_p.at[h, k],
+            (f, chip_at(k) * 2 + core),
+        )
+
+    for h in range(SIDES):
+        swap_g(h).wait_recv()
+        half_g[:, sides[h]] = gram[mine, sides[h]] + core_g[:, sides[h]]
+        for k in NEXT:
+            scatter_g(h, k).start()
 
     each(peers, scatter_y, arrived)
     total = part_y[core, chip]
@@ -245,16 +258,24 @@
 
     each(zs, z_send_y, started)
 
-    each(NEXT, scatter_g, arrived)
-    total = half_g[pl.ds(pl.multiple_of(chip * SLAB, SLAB), SLAB)]
-    for k in NEXT:
-        total = total + plane_g[k]
-    slab_g[...] = total
-
-    def z_send_g(i):
-        return to_z(slab_g, z_g.at[i], 1, i)
-
-    each(zs, z_send_g, started)
+    def z_send_g(h, i):
+        return to_z(
+            slab_g.at[:, sides[h]], z_g.at[i, :, sides[h]], 1 + h, i
+        )
+
+    def on_to_z(h):
+        own = pl.ds(pl.multiple_of(chip * SLAB, SLAB), SLAB)
+        total = half_g[own, sides[h]]
+        for k in NEXT:
+            scatter_g(h, k).wait_recv()
+        for k in NEXT:
+            total = total + plane_g[k, :, sides[h]]
+        slab_g[:, sides[h]] = total
+        for i in zs:
+            z_send_g(h, i).start()
+
+    on_to_z(0)
+    on_to_z(1)
 
     def z_sum(own, of):
         acc = None
@@ -279,7 +300,9 @@
     each(peers, gather_y, arrived)
     y1 = unpack(y_all[...].reshape(2 * CHIPS, 8, LANES))
 
-    each(zs, z_send_g, arrived)
+    for h in range(SIDES):
+        for i in zs:
+            z_send_g(h, i).wait_recv()
     own_g = z_sum(slab_g[...], z_g)
     own_y[2] = pack(dot(own_g, y1, ((1,), (0,))))[0]
     each(peers, gather_w, started)
@@ -306,10 +329,13 @@
 
     for make in (scatter_y, gather_y, gather_w):
         each(peers, make, left)
-    for make in (z_send_y, z_send_g):
-        each(zs, make, left)
-    each(NEXT, scatter_g, left)
-    swap_g.wait_send()
+    each(zs, z_send_y, left)
+    for h in range(SIDES):
+        swap_g(h).wait_send()
+        for k in NEXT:
+            scatter_g(h, k).wait_send()
+        for i in zs:
+            z_send_g(h, i).wait_send()
 
 
 def shards(tensor, initial):
@@ -340,14 +366,14 @@
             pltpu.SemaphoreType.DMA((CHUNKS,)),
             pltpu.SemaphoreType.DMA((CHUNKS, NZ - 1)),
             pltpu.SemaphoreType.DMA((CHUNKS, NZ - 1)),
-            pltpu.SemaphoreType.DMA((CHIPS,)),
-            pltpu.SemaphoreType.DMA((CHIPS,)),
+            pltpu.SemaphoreType.DMA((SIDES, CHIPS)),
+            pltpu.SemaphoreType.DMA((SIDES, CHIPS)),
             pltpu.SemaphoreType.DMA((3, len(PEERS))),
             pltpu.SemaphoreType.DMA((3, len(PEERS))),
-            pltpu.SemaphoreType.DMA((2, NZ - 1)),
-            pltpu.SemaphoreType.DMA((2, NZ - 1)),
-            pltpu.SemaphoreType.DMA((1,)),
-            pltpu.SemaphoreType.DMA((1,)),
+            pltpu.SemaphoreType.DMA((1 + SIDES, NZ - 1)),
+            pltpu.SemaphoreType.DMA((1 + SIDES, NZ - 1)),
+            pltpu.SemaphoreType.DMA((SIDES,)),
+            pltpu.SemaphoreType.DMA((SIDES,)),
         ],
         compiler_params=pltpu.CompilerParams(
             collective_id=0, has_side_effects=True, vmem_limit_bytes=51 * 1024 * 1024

time: 141 us -> 140 us (level)
  Pallas kernels: 138 us -> 136 us
    pallas_call x1, Pallas kernels: 138 us -> 136 us  [shards(): pl.pallas_call(kernel, name='subspace', out_shape=(jax.ShapeDtypeStruct((...]
where the time goes in v5:
time: 140 us
  Pallas kernels  136 us (97%)
  local copies, waits for them, and re-layouts  2.89 us (2%)
    pallas_call x1, Pallas kernels, shards(): pl.pallas_call(kernel, name='subspace', out_shape=(jax.ShapeDtypeStruct((...  136 us
    unnamed x4, local copies, waits for them, and re-layouts  2.89 us

profile of v5, /device:TPU:1, one launch (start us, length us, event | category | flops | bytes accessed | tf_op | source)
XLA Modules:
  0.0 139.8 jit_solution(7031046158386085686)
XLA Ops:
  0.6 0.0 copy-start
  0.6 0.9 copy-done
  1.5 136.3 %subspace.1 = (f32[64,2048]{1,0:T(8,128)S(1)}, f32[64,512]{1,0:T(8,128)S(1)}) custom-call(f32[64,1,8,2048]{3,2,1,0:T(8,128)} %tensor.1, f32[64,512]{1,0:T(8,128)S(1)} %bitcast.4), custom_call_target="tpu_custom_call" | custom-call | tf_op jit(solution)/shard_map/subspace/pallas_call | solution.py:343
  137.8 1.3 copy.4
  139.2 0.7 copy.6
Async XLA Ops:
  0.6 0.9 copy-start

commit v6 on v5

--- a/solution.py
+++ b/solution.py
@@ -274,6 +274,11 @@
         for i in zs:
             z_send_g(h, i).start()
 
+    @pl.loop(0, CHUNKS)
+    def _(j):
+        for i in range(NZ - 1):
+            exchange(j, i).wait_send()
+
     on_to_z(0)
     on_to_z(1)
 
@@ -297,6 +302,13 @@
 
     each(peers, gather_y, started)
     y_all[core, chip] = own_y[1]
+    each(peers, scatter_y, left)
+    each(zs, z_send_y, left)
+    for h in range(SIDES):
+        swap_g(h).wait_send()
+        for k in NEXT:
+            scatter_g(h, k).wait_send()
+
     each(peers, gather_y, arrived)
     y1 = unpack(y_all[...].reshape(2 * CHIPS, 8, LANES))
 
@@ -309,6 +321,11 @@
     w_all[core, chip] = own_y[2]
     squares = dot(y1, y1, ((0,), (0,)))
     inverse1 = inverse_factor(jnp.concatenate([squares, squares], axis=1))
+    each(peers, gather_y, left)
+    for h in range(SIDES):
+        for i in zs:
+            z_send_g(h, i).wait_send()
+
     each(peers, gather_w, arrived)
 
     w = unpack(w_all[...].reshape(2 * CHIPS, 8, LANES))
@@ -320,22 +337,11 @@
 
     for j in range(0, CHUNKS, 2):
         pair = jnp.concatenate([x[j].reshape(M, CW), x[j + 1].reshape(M, CW)], axis=1)
-        slab_out[:, j * CW : (j + 2) * CW] = dot(basis, pair, ((1,), (0,)))
-
-    @pl.loop(0, CHUNKS)
-    def _(j):
-        for i in range(NZ - 1):
-            exchange(j, i).wait_send()
-
-    for make in (scatter_y, gather_y, gather_w):
-        each(peers, make, left)
-    each(zs, z_send_y, left)
-    for h in range(SIDES):
-        swap_g(h).wait_send()
-        for k in NEXT:
-            scatter_g(h, k).wait_send()
-        for i in zs:
-            z_send_g(h, i).wait_send()
+        columns = dot(basis, pair, ((1,), (0,)))
+        slab_out[:, j, :] = columns[:, :CW]
+        slab_out[:, j + 1, :] = columns[:, CW:]
+
+    each(peers, gather_w, left)
 
 
 def shards(tensor, initial):
@@ -344,7 +350,7 @@
         kernel,
         name="subspace",
         out_shape=(
-            jax.ShapeDtypeStruct((RANK, WIDTH), F32),
+            jax.ShapeDtypeStruct((RANK, CHUNKS, CW), F32),
             jax.ShapeDtypeStruct((RANK, M), F32),
         ),
         in_specs=[pl.BlockSpec(memory_space=pl.ANY), vmem],

time: 140 us -> 139 us (level)
  no operation moved by 1% of the time
where the time goes in v6:
time: 139 us
  Pallas kernels  136 us (98%)
  local copies, waits for them, and re-layouts  2.35 us (2%)
    pallas_call x1, Pallas kernels, shards(): pl.pallas_call(kernel, name='subspace', out_shape=(jax.ShapeDtypeStruct((...  136 us

profile of v6, /device:TPU:1, one launch (start us, length us, event | category | flops | bytes accessed | tf_op | source)
XLA Modules:
  0.0 139.1 jit_solution(7670627003359920982)
XLA Ops:
  0.6 0.0 copy-start
  0.6 0.9 copy-done
  1.5 136.1 %subspace.1 = (f32[64,16,128]{2,1,0:T(8,128)S(1)}, f32[64,512]{1,0:T(8,128)S(1)}) custom-call(f32[64,1,8,2048]{3,2,1,0:T(8,128)} %tensor.1, f32[64,512]{1,0:T(8,128)S(1)} %bitcast.4), custom_call_target="tpu_custom_call" | custom-call | tf_op jit(solution)/shard_map/subspace/pallas_call | solution.py:349
  137.6 0.8 copy.7
  138.4 0.7 copy.8
Async XLA Ops:
  0.6 0.9 copy-start

commit v7 on v6

--- a/solution.py
+++ b/solution.py
@@ -36,6 +36,11 @@
     return lax.dot_general(
         a, b, (contract, ((), ())), precision=HIGHEST, preferred_element_type=F32
     )
+
+
+def halves(value):
+    high = value.astype(jnp.bfloat16)
+    return high, (value - high.astype(F32)).astype(jnp.bfloat16)
 
 
 def augmented(squares):
@@ -335,9 +340,16 @@
     basis = dot(inverse2, y2, ((1,), (0,)))
     basis_out[...] = basis
 
+    high, low = halves(basis)
+    left_side = jnp.concatenate([high, high, low], axis=1)
     for j in range(0, CHUNKS, 2):
         pair = jnp.concatenate([x[j].reshape(M, CW), x[j + 1].reshape(M, CW)], axis=1)
-        columns = dot(basis, pair, ((1,), (0,)))
+        high, low = halves(pair)
+        columns = jnp.dot(
+            left_side,
+            jnp.concatenate([high, low, high], axis=0),
+            preferred_element_type=F32,
+        )
         slab_out[:, j, :] = columns[:, :CW]
         slab_out[:, j + 1, :] = columns[:, CW:]
 

time: 139 us -> 139 us (level)
  no operation moved by 1% of the time
where the time goes in v7:
time: 139 us
  Pallas kernels  136 us (98%)
  local copies, waits for them, and re-layouts  2.35 us (2%)
    pallas_call x1, Pallas kernels, shards(): pl.pallas_call(kernel, name='subspace', out_shape=(jax.ShapeDtypeStruct((...  136 us

profile of v7, /device:TPU:1, one launch (start us, length us, event | category | flops | bytes accessed | tf_op | source)
XLA Modules:
  0.0 138.9 jit_solution(12073222778185530670)
XLA Ops:
  0.6 0.0 copy-start
  0.6 0.9 copy-done
  1.5 135.9 %subspace.1 = (f32[64,16,128]{2,1,0:T(8,128)S(1)}, f32[64,512]{1,0:T(8,128)S(1)}) custom-call(f32[64,1,8,2048]{3,2,1,0:T(8,128)} %tensor.1, f32[64,512]{1,0:T(8,128)S(1)} %bitcast.4), custom_call_target="tpu_custom_call" | custom-call | tf_op jit(solution)/shard_map/subspace/pallas_call | solution.py:361
  137.4 0.8 copy.7
  138.2 0.7 copy.8
Async XLA Ops:
  0.6 0.9 copy-start
